TPU v7x, 32 devices: a whole 2x2x4 slice. The times are simulated.
32 devices in a mesh: ga: 4 (over z), sa: 8 (over y, x, core).
Axes of the slice: x: 2, y: 2, z: 4, core: 2. Of those that a mesh axis runs over, the one named last changes fastest.
Arguments:
- slab: float32 [8, 64, 64, 512], P(None, None, 'sa', 'ga'), may hold values from -6 to 6
- factor: float32 [64, 64], P('sa'), may hold values from -0.75 to 0.75
Outputs:
- lower: float32 [512, 512], P('ga')
- basis: float32 [8, 64, 64, 512], P('ga', 'sa')
All inputs are finite; a program needn't handle non-finite values.
Results may differ from a plain program's by a relative error of at most 0.000073.
Values sent between devices are 32-bit elements; how exact they have to be, the bound alone decides.
A program may use at most 128 MiB of HBM per device.

v0:
```python
import jax
import jax.numpy as jnp
from jax import lax
from jax.sharding import PartitionSpec as P

S = 8
R1 = 64
R2 = 64


def shards(slab, factor):
    whole_factor = lax.all_gather(factor, "sa", axis=0, tiled=True)
    regrouped = lax.all_to_all(slab, "sa", split_axis=1, concat_axis=2, tiled=True)
    proj = jnp.einsum("sajk,jr->sark", regrouped, whole_factor, precision=lax.Precision.HIGHEST)
    fibres = lax.all_to_all(proj, "ga", split_axis=0, concat_axis=3, tiled=True)
    order = fibres.shape[3]
    columns = fibres.reshape(-1, order)
    gram_part = jnp.dot(
        columns.T, columns, precision=lax.Precision.HIGHEST, preferred_element_type=jnp.float32
    )
    gram = lax.psum(gram_part, ("ga", "sa")) / (S * R1 * R2)
    lower = jnp.linalg.cholesky(gram)
    solved = jax.scipy.linalg.solve_triangular(lower, columns.T, lower=True)
    basis = solved.T.reshape(fibres.shape)
    rows_here = order // lax.axis_size("ga")
    start = lax.axis_index("ga") * rows_here
    lower_rows = lax.dynamic_slice_in_dim(lower, start, rows_here, 0)
    return (lower_rows, basis)


def solution(mesh):
    placed = (P(None, None, "sa", "ga"), P("sa", None))
    return jax.shard_map(
        shards,
        mesh=mesh,
        in_specs=placed,
        out_specs=(P("ga", None), P("ga", "sa", None, None)),
        check_vma=False,
    )
```

profile of v0, /device:TPU:0, one launch (start us, length us, event | category | flops | bytes accessed | tf_op | source)
XLA Modules:
  0.0 403.1 jit_solution(13747476337796545025)
XLA Ops:
  7.2 3.2 copy.13
  10.4 0.0 copy-start.2
  10.4 5.3 %all-to-all-start = ((f32[8,64,8,128]{3,2,0,1:T(8,128)}), f32[8,64,8,128]{3,2,0,1:T(8,128)S(1)}, u32[]{:S(2)}, u32[]{:S(2)}) async-start(f32[8,64,8,128]{3,2,0,1:T(8,128)} %copy.13), calls=%async_computation | async-start | bytes 4194304 | tf_op jit(solution)/shard_map/all_to_all | solution.py:13
  15.7 0.0 all-reduce.3.cloned.1.call-start
  15.7 0.0 copy-done.2
  15.7 29.8 %all_gather.3 = f32[64,64]{1,0:T(8,128)S(1)} all-gather(f32[8,64]{1,0:T(8,128)S(1)} %copy-done.2), channel_id=1, replica_groups=mesh['ga'=4,'sa'=8] {'sa'}, dimensions={0}, use_global_device_ids=true | all-gather | bytes 18432 | tf_op jit(solution)/shard_map/all_gather | solution.py:12
  45.5 0.0 all-to-all-done
  45.5 1.9 fusion.3
  47.5 53.4 %all_to_all.33 = f32[8,8,64,128]{3,2,1,0:T(8,128)S(1)} all-to-all(f32[8,8,64,128]{3,2,1,0:T(8,128)S(1)} %fusion.3), channel_id=1, replica_groups=mesh['ga'=4,'sa'=8] {'ga'}, dimensions={0} | all-to-all | bytes 4194304 | tf_op jit(solution)/shard_map/all_to_all | solution.py:15
  100.8 1.4 copy.15
  102.2 4.6 %fusion.42 = f32[512,512]{0,1:T(8,128)} fusion(f32[128,8,4,128]{3,2,1,0:T(4,128)S(1)} %bitcast.79), kind=kOutput, calls=%fused_computation.76 | convolution fusion | flops 3221225472 | bytes 3145728 | tf_op jit(solution)/shard_map/dot_general | solution.py:18
  106.8 0.0 all-reduce.3.cloned.1.call-update
  106.9 1.5 copy.31
  108.4 2.2 copy.18
  110.5 123.5 %all-reduce.3.cloned.1.call-done = f32[512,512]{0,1:T(8,128)} async-done(((f32[512,512]{0,1:T(8,128)}), f32[512,512]{0,1:T(8,128)}) %all-reduce.3.cloned.1.call-update) | async-done | bytes 1048592 | tf_op jit(solution)/shard_map/psum | solution.py:21
  234.1 0.0 copy-start
  234.1 2.4 broadcast_multiply_fusion
  236.5 2.6 copy.17
  239.1 0.0 copy-done
  239.1 1.5 fusion.18
  240.5 0.0 copy-start.1
  240.5 1.0 copy-done.1
  241.5 11.7 %cholesky.104 = f32[128,128]{1,0:T(8,128)S(1)} custom-call(f32[128,128]{1,0:T(8,128)S(1)} %cholesky.266), custom_call_target="Cholesky" | custom-call | tf_op jit(solution)/shard_map/jit(cholesky)/cholesky | solution.py:22
  253.2 0.1 cholesky.224
  253.4 9.8 %custom-call.31 = f32[1,128,128]{1,2,0:T(8,128)S(1)} custom-call(f32[1,128,128]{2,1,0:T(8,128)S(1)} %get-tuple-element.33), custom_call_target="InvertDiagBlocksLowerTriangular" | custom-call | tf_op jit(solution)/shard_map/jit(cholesky)/cholesky | solution.py:22
  263.2 1.2 constant_dynamic-update-slice_fusion.3
  264.4 1.3 convolution_subtract_fusion.2
  265.7 11.7 %cholesky.217 = f32[128,128]{1,0:T(8,128)S(1)} custom-call(f32[128,128]{1,0:T(8,128)S(1)} %cholesky.270), custom_call_target="Cholesky" | custom-call | tf_op jit(solution)/shard_map/jit(cholesky)/cholesky | solution.py:22
  277.5 10.0 %custom-call.32 = f32[1,128,128]{1,2,0:T(8,128)S(1)} custom-call(f32[1,128,128]{2,1,0:T(8,128)S(1)} %get-tuple-element.30), custom_call_target="InvertDiagBlocksLowerTriangular" | custom-call | tf_op jit(solution)/shard_map/jit(cholesky)/cholesky | solution.py:22
  287.5 0.3 convolution_dynamic-update-slice_fusion
  287.7 1.3 convolution_subtract_fusion.3
  289.0 11.7 %cholesky.238 = f32[128,128]{1,0:T(8,128)S(1)} custom-call(f32[128,128]{1,0:T(8,128)S(1)} %cholesky.275), custom_call_target="Cholesky" | custom-call | tf_op jit(solution)/shard_map/jit(cholesky)/cholesky | solution.py:22
  300.8 9.8 %custom-call.33 = f32[1,128,128]{1,2,0:T(8,128)S(1)} custom-call(f32[1,128,128]{2,1,0:T(8,128)S(1)} %get-tuple-element.27), custom_call_target="InvertDiagBlocksLowerTriangular" | custom-call | tf_op jit(solution)/shard_map/jit(cholesky)/cholesky | solution.py:22
  310.6 0.2 convolution_dynamic-update-slice_fusion.1
  310.8 1.2 convolution_subtract_fusion.4
  312.1 11.7 %cholesky.255 = f32[128,128]{1,0:T(8,128)S(1)} custom-call(f32[128,128]{1,0:T(8,128)S(1)} %convolution_subtract_fusion.4), custom_call_target="Cholesky" | custom-call | tf_op jit(solution)/shard_map/jit(cholesky)/cholesky | solution.py:22
  323.8 0.7 compare_reduce_fusion.1
  324.5 0.6 compare_reduce_fusion
  325.1 0.9 compare_reduce_fusion.2
  328.6 1.6 fusion.19
  330.2 14.1 %while.1 = (s32[]{:T(128)}, f32[512,512]{1,0:T(8,128)}, s32[4,2]{0,1:T(2,128)S(1)}, f32[4,128,128]{2,1,0:T(8,128)}, s32[]{:T(128)}) while((s32[]{:T(128)}, f32[512,512]{1,0:T(8,128)}, s32[4,2]{0,1:T(2,128)S(1)}, f32[4,128,128]{2,1,0:T(8,128)}, s32[]{:T(128)}) %tuple.33), condition=%wide.while_cond, body=%wide.while_body.sunk | while | flops 2 | bytes 132205 | solution.py:23
  330.2 0.1 constant_dynamic-slice_fusion.3
  330.3 0.6 fusion.50
  330.9 2.9 bitcast_dynamic-update-slice_fusion.2
  333.7 0.1 constant_dynamic-slice_fusion.3
  333.8 0.6 fusion.50
  334.4 2.9 bitcast_dynamic-update-slice_fusion.2
  337.3 0.1 constant_dynamic-slice_fusion.3
  337.4 0.6 fusion.50
  338.0 2.9 bitcast_dynamic-update-slice_fusion.2
  340.8 0.1 constant_dynamic-slice_fusion.3
  340.9 0.6 fusion.50
  341.5 2.8 bitcast_dynamic-update-slice_fusion.2
  344.3 40.1 %custom-call.34 = f32[4,128,128]{1,2,0:T(8,128)S(1)} custom-call(f32[4,128,128]{2,1,0:T(8,128)} %get-tuple-element.9), custom_call_target="InvertDiagBlocksLowerTriangular" | custom-call | tf_op jit(solution)/shard_map/jit(_solve_triangular)/triangular_solve | solution.py:23
  384.5 0.6 fusion.20
  385.1 1.4 convolution_subtract_fusion.1
  386.5 0.6 fusion.33
  387.2 1.6 convolution_subtract_fusion
  388.8 0.6 fusion.31
  389.4 2.0 fusion.12
  391.5 0.6 fusion.30
  392.1 0.2 maximum_bitcast_fusion
  392.4 1.8 copy.19
  394.2 1.7 constant_dynamic-slice_fusion.1
  (10 shorter events, 0.2 us)
Async XLA Ops:
  10.4 5.4 %copy-start.2 = (f32[8,64]{1,0:T(8,128)S(1)}, f32[8,64]{1,0:T(8,128)}, u32[]{:S(2)}) copy-start(f32[8,64]{1,0:T(8,128)} %param.3) | copy-start | bytes 6148
  10.4 35.2 %all-to-all-start = ((f32[8,64,8,128]{3,2,0,1:T(8,128)}), f32[8,64,8,128]{3,2,0,1:T(8,128)S(1)}, u32[]{:S(2)}, u32[]{:S(2)}) async-start(f32[8,64,8,128]{3,2,0,1:T(8,128)} %copy.13), calls=%async_computation | async-start | bytes 4194304 | tf_op jit(solution)/shard_map/all_to_all | solution.py:13
  15.7 218.4 %all-reduce.3.cloned.1.call-start = ((), (), s32[]{:S(2)}) async-start(), calls=%async_computation.2 | async-start | bytes 2097152 | tf_op jit(solution)/shard_map/psum | solution.py:21
  234.1 5.0 %copy-start = (f32[512,512]{0,1:T(8,128)S(1)}, f32[512,512]{0,1:T(8,128)}, u32[]{:S(2)}) copy-start(f32[512,512]{0,1:T(8,128)} %all-reduce.3.cloned.1.call-done) | copy-start | bytes 3145732
  240.5 1.0 copy-start.1
Sparse Core Ops, SparseCore 0:
  107.0 127.0 all-reduce.2
where the time goes:
time: 410 us; the launch traced here: 403 us
  other arithmetic  125 us (30%)
  waiting for transfers between devices  124 us (30%)
  blocking collectives  83.2 us (20%)
  local copies, waits for them, and re-layouts  29.6 us (7%)
  matrix products  19.6 us (5%)
  between operations  17.2 us (4%)
  starting transfers between devices  5.34 us (1%)
    psum x1, waiting for transfers between devices, shards(): gram = lax.psum(gram_part, ('ga', 'sa')) / (S * R1 * R2)  124 us
    another operation x14, other arithmetic, shards(): lower = jnp.linalg.cholesky(gram)  78.9 us
    all_to_all x1, blocking collectives, shards(): fibres = lax.all_to_all(proj, 'ga', split_axis=0, concat_axis=3, tiled=True)  53.4 us
    another operation x3, other arithmetic, shards(): solved = jax.scipy.linalg.solve_triangular(lower, columns.T, lower=True)  41.7 us
    all_gather x1, blocking collectives, shards(): whole_factor = lax.all_gather(factor, 'sa', axis=0, tiled=True)  29.8 us
    another operation x12, local copies, waits for them, and re-layouts  14.1 us
  transfers between devices with their start and end apart: 2, of which 1 were waited for; matrix products, arithmetic and copies ran while one was open for 1% of the time, Pallas kernels for 0%

commit v1 on v0

v1 whole, which is shorter than its diff:
```python
import functools

import jax
import jax.numpy as jnp
from jax import lax
from jax.experimental import pallas as pl
from jax.experimental.pallas import tpu as pltpu
from jax.sharding import PartitionSpec as P

MESH = pl.DeviceIdType.MESH
HIGHEST = lax.Precision.HIGHEST
LANES = 128
HALF = 64
STEP = 4


def tn(a, b):
    return lax.dot_general(a, b, (((0,), (0,)), ((), ())), precision=HIGHEST, preferred_element_type=jnp.float32)


def nn(a, b):
    return lax.dot_general(a, b, (((1,), (0,)), ((), ())), precision=HIGHEST, preferred_element_type=jnp.float32)


def split(x):
    hi = x.astype(jnp.bfloat16)
    return hi, (x - hi.astype(jnp.float32)).astype(jnp.bfloat16)


def mul16(a, b, dims):
    return lax.dot_general(a, b, (dims, ((), ())), preferred_element_type=jnp.float32)


def exchange_kernel(
    G, C, count,
    slab, factor, unfold, gram,
    fibres, whole_factor, acc, r1, s1, r2, s2, r3,
    a2a_send, a2a_recv, f_send, f_recv, own_sem,
    p1_send, p1_recv, p2_send, p2_recv, p3_send, p3_recv,
    g1_send, g1_recv, g2_send, g2_recv, g3_send, g3_recv,
):
    g, c = lax.axis_index("ga"), lax.axis_index("sa")
    D, chips = G * C, C // 2
    me = g * C + c
    core, chip = lax.rem(c, 2), c // 2
    s_here, a_here, depth, order = fibres.shape
    j_here, k_here = slab.shape[2], slab.shape[3]

    barrier = pltpu.get_barrier_semaphore()

    @pl.loop(1, D)
    def _(d):
        to = lax.rem(me + d, D)
        pl.semaphore_signal(barrier, inc=1, device_id=(to // C, lax.rem(to, C)), device_id_type=MESH)

    pl.semaphore_wait(barrier, D - 1)

    def remote(src, dst, send, recv, device):
        return pltpu.make_async_remote_copy(
            src_ref=src, dst_ref=dst, send_sem=send, recv_sem=recv, device_id=device, device_id_type=MESH
        )

    j_rows = pl.ds(pl.multiple_of(c * j_here, j_here), j_here)
    k_cols = pl.ds(pl.multiple_of(g * k_here, k_here), k_here)

    def factor_copy(d):
        return remote(factor, whole_factor.at[j_rows, :], f_send.at[d], f_recv.at[d], (g, lax.rem(c + d, C)))

    def chunk(to):
        return slab.at[pl.ds((to // C) * s_here, s_here), pl.ds(lax.rem(to, C) * a_here, a_here)]

    def slab_copy(d):
        to = lax.rem(me + d, D)
        return remote(
            chunk(to), fibres.at[:, :, j_rows, k_cols], a2a_send.at[d], a2a_recv.at[d], (to // C, lax.rem(to, C))
        )

    @pl.loop(1, C)
    def _(d):
        factor_copy(d).start()

    @pl.loop(1, D)
    def _(d):
        slab_copy(d).start()

    own = pltpu.make_async_copy(chunk(me), fibres.at[:, :, j_rows, k_cols], own_sem)
    own.start()
    whole_factor[j_rows, :] = factor[...]
    own.wait()

    @pl.loop(1, C)
    def _(d):
        factor_copy(d).wait()

    @pl.loop(1, D)
    def _(d):
        slab_copy(d).wait()

    @pl.loop(0, s_here * a_here)
    def _(i):
        s, a = i // a_here, lax.rem(i, a_here)
        unfold[s, a] = tn(whole_factor[...], fibres[s, a])

    columns = unfold[...].reshape(s_here * a_here * unfold.shape[2], order)
    hi, lo = split(columns)
    at = 0
    for left in range(0, order, LANES):
        low_hi, low_lo = hi[:, left:], lo[:, left:]
        this_hi, this_lo = hi[:, left:left + LANES], lo[:, left:left + LANES]
        contract = ((0,), (0,))
        part = mul16(low_hi, this_lo, contract) + mul16(low_lo, this_hi, contract)
        part = part + mul16(low_hi, this_hi, contract)
        acc[at:at + order - left, :] = part
        at += order - left
    if at < acc.shape[0]:
        acc[at:, :] = jnp.zeros((acc.shape[0] - at, LANES), jnp.float32)

    half, quarter = s1.shape[0], s2.shape[0]
    eighth = quarter // G

    def rows(start, size):
        return pl.ds(pl.multiple_of(start, 8), size)

    partner = (g, c + 1 - 2 * core)
    swap = remote(acc.at[rows((1 - core) * half, half)], r1, p1_send, p1_recv, partner)
    swap.start()
    swap.wait()
    s1[...] = acc[rows(core * half, half), :] + r1[...]

    def plane(d):
        to = lax.rem(chip + d, chips)
        return remote(s1.at[rows(to * quarter, quarter)], r2.at[d], p2_send.at[d], p2_recv.at[d], (g, to * 2 + core))

    for d in range(1, chips):
        plane(d).start()
    for d in range(1, chips):
        plane(d).wait()
    total = s1[rows(chip * quarter, quarter), :]
    for d in range(1, chips):
        total = total + r2[d]
    s2[...] = total

    def line(d):
        to = lax.rem(g + d, G)
        return remote(s2.at[rows(to * eighth, eighth)], r3.at[d], p3_send.at[d], p3_recv.at[d], (to, c))

    for d in range(1, G):
        line(d).start()
    for d in range(1, G):
        line(d).wait()
    total = s2[rows(g * eighth, eighth), :]
    for d in range(1, G):
        total = total + r3[d]
    mine = rows(core * half + chip * quarter + g * eighth, eighth)
    gram[mine, :] = total / count

    def line_back(d):
        return remote(gram.at[mine], gram.at[mine], g1_send.at[d], g1_recv.at[d], (lax.rem(g + d, G), c))

    for d in range(1, G):
        line_back(d).start()
    for d in range(1, G):
        line_back(d).wait()
    mine2 = rows(core * half + chip * quarter, quarter)

    def plane_back(d):
        to = lax.rem(chip + d, chips)
        return remote(gram.at[mine2], gram.at[mine2], g2_send.at[d], g2_recv.at[d], (g, to * 2 + core))

    for d in range(1, chips):
        plane_back(d).start()
    for d in range(1, chips):
        plane_back(d).wait()
    mine3 = rows(core * half, half)
    swap_back = remote(gram.at[mine3], gram.at[mine3], g3_send, g3_recv, partner)
    swap_back.start()
    swap_back.wait()


def eliminate(block):
    at_row = lax.broadcasted_iota(jnp.int32, (HALF, LANES), 0)
    at_lane = lax.broadcasted_iota(jnp.int32, (HALF, LANES), 1)
    m = jnp.concatenate([block, jnp.zeros((HALF, HALF), jnp.float32)], axis=1)
    m = jnp.where(at_lane == at_row + HALF, 1.0, m)
    for j in range(0, HALF, STEP):
        cols = [jnp.broadcast_to(m[:, j + t:j + t + 1], (HALF, LANES)) for t in range(STEP)]
        lines = [m[j + t:j + t + 1, :] for t in range(STEP)]
        small = [[cols[u][j + t:j + t + 1, :] for u in range(STEP)] for t in range(STEP)]
        for t in range(STEP):
            inverse = 1.0 / small[t][t]
            for u in range(t + 1, STEP):
                ratio = small[t][u] * inverse
                lines[u] = lines[u] - ratio * lines[t]
                cols[u] = cols[u] - ratio * cols[t]
                for v in range(u, STEP):
                    small[u][v] = small[u][v] - ratio * small[t][v]
            m = m - jnp.where(at_row > j + t, cols[t] * inverse, 0.0) * lines[t]
    pivot = jnp.sum(jnp.where(at_lane == at_row, m, 0.0), axis=1, keepdims=True)
    m = m * lax.rsqrt(pivot)
    upper = jnp.where(at_lane >= at_row, m, 0.0)
    return upper[:, :HALF], m[:, HALF:]


def factor_128(a):
    u1, w1 = eliminate(a[:HALF, :HALF])
    u12 = nn(w1, a[:HALF, HALF:])
    u2, w2 = eliminate(a[HALF:, HALF:] - tn(u12, u12))
    w21 = -nn(w2, tn(u12, w1))
    zero = jnp.zeros((HALF, HALF), jnp.float32)
    u = jnp.concatenate([jnp.concatenate([u1, u12], 1), jnp.concatenate([zero, u2], 1)], 0)
    w = jnp.concatenate([jnp.concatenate([w1, zero], 1), jnp.concatenate([w21, w2], 1)], 0)
    return u, w


def solve_kernel(unfold, gram, lower, basis, upper, inverse):
    order = upper.shape[0]
    upper[...] = jnp.zeros_like(upper)
    inverse[...] = jnp.zeros_like(inverse)
    at = 0
    for left in range(0, order, LANES):
        tall = gram[at:at + order - left, :]
        upper[left:left + LANES, left:] = tall.T
        at += order - left
    for i in range(0, order, LANES):
        n = i + LANES
        u, w = factor_128(upper[i:n, i:n])
        upper[i:n, i:n] = u
        if i:
            inverse[i:n, :i] = nn(w, inverse[i:n, :i])
        inverse[i:n, i:n] = w
        if n < order:
            right = nn(w, upper[i:n, n:])
            upper[i:n, n:] = right
            for t in range(n, order, LANES):
                block = right[:, t - n:t - n + LANES]
                upper[t:t + LANES, t:] -= tn(block, right[:, t - n:])
                inverse[t:t + LANES, :n] -= tn(block, inverse[i:n, :n])
    g = lax.axis_index("ga")
    mine = lower.shape[0]
    lower[...] = upper[:, pl.ds(pl.multiple_of(g * mine, mine), mine)].T
    w_hi, w_lo = split(inverse[...])
    contract = ((1,), (1,))

    @pl.loop(0, basis.shape[0] // LANES)
    def _(r):
        here = pl.ds(pl.multiple_of(r * LANES, LANES), LANES)
        hi, lo = split(unfold[here, :])
        out = mul16(hi, w_lo, contract) + mul16(lo, w_hi, contract)
        basis[here, :] = out + mul16(hi, w_hi, contract)


def shards(G, C, slab, factor):
    S, A, j_here, k_here = slab.shape
    R = factor.shape[1]
    depth, order = j_here * C, k_here * G
    s_here, a_here, chips = S // G, A // C, C // 2
    blocks = order // LANES
    cut = 8 * 2 * chips * G
    packed = -(-(blocks * (blocks + 1) // 2 * LANES) // cut) * cut
    half, quarter = packed // 2, packed // 2 // chips
    f32 = jnp.float32
    dma = pltpu.SemaphoreType.DMA
    unfold, gram = pl.pallas_call(
        functools.partial(exchange_kernel, G, C, S * A * R),
        out_shape=(
            jax.ShapeDtypeStruct((s_here, a_here, R, order), f32),
            jax.ShapeDtypeStruct((packed, LANES), f32),
        ),
        in_specs=[pl.BlockSpec(memory_space=pl.ANY), pl.BlockSpec(memory_space=pltpu.VMEM)],
        out_specs=(pl.BlockSpec(memory_space=pltpu.VMEM), pl.BlockSpec(memory_space=pltpu.VMEM)),
        scratch_shapes=[
            pltpu.VMEM((s_here, a_here, depth, order), f32),
            pltpu.VMEM((depth, R), f32),
            pltpu.VMEM((packed, LANES), f32),
            pltpu.VMEM((half, LANES), f32),
            pltpu.VMEM((half, LANES), f32),
            pltpu.VMEM((chips, quarter, LANES), f32),
            pltpu.VMEM((quarter, LANES), f32),
            pltpu.VMEM((G, quarter // G, LANES), f32),
            dma((G * C,)), dma((G * C,)), dma((C,)), dma((C,)), dma,
            dma, dma, dma((chips,)), dma((chips,)), dma((G,)), dma((G,)),
            dma((G,)), dma((G,)), dma((chips,)), dma((chips,)), dma, dma,
        ],
        compiler_params=pltpu.CompilerParams(
            collective_id=0, has_side_effects=True, vmem_limit_bytes=40 * 1024 * 1024
        ),
    )(slab, factor)
    rows = s_here * a_here * R
    lower, basis = pl.pallas_call(
        solve_kernel,
        out_shape=(
            jax.ShapeDtypeStruct((order // G, order), f32),
            jax.ShapeDtypeStruct((rows, order), f32),
        ),
        in_specs=[pl.BlockSpec(memory_space=pltpu.VMEM)] * 2,
        out_specs=(pl.BlockSpec(memory_space=pltpu.VMEM), pl.BlockSpec(memory_space=pltpu.VMEM)),
        scratch_shapes=[pltpu.VMEM((order, order), f32), pltpu.VMEM((order, order), f32)],
        compiler_params=pltpu.CompilerParams(vmem_limit_bytes=40 * 1024 * 1024),
    )(unfold.reshape(rows, order), gram)
    return lower, basis.reshape(s_here, a_here, R, order)


def solution(mesh):
    placed = (P(None, None, "sa", "ga"), P("sa", None))
    return jax.shard_map(
        functools.partial(shards, mesh.shape["ga"], mesh.shape["sa"]),
        mesh=mesh,
        in_specs=placed,
        out_specs=(P("ga", None), P("ga", "sa", None, None)),
        check_vma=False,
    )
```

time: 410 us -> 116 us (0.28); the launches traced: 403 us -> 116 us
  other arithmetic: 125 us -> 0 us
  waiting for transfers between devices: 124 us -> 0 us
  Pallas kernels: 0 us -> 113 us
  blocking collectives: 83.2 us -> 0 us
  local copies, waits for them, and re-layouts: 29.6 us -> 2.27 us
  matrix products: 19.6 us -> 0 us
  between operations: 17.2 us -> 0.65 us
  starting transfers between devices: 5.34 us -> 0 us
    psum x1 -> x0, waiting for transfers between devices: 124 us -> none  [shards(): gram = lax.psum(gram_part, ('ga', 'sa')) / (S * R1 * R2)]
    another operation x17 -> x0, other arithmetic: 121 us -> none  [the longest x14 78.9 us: shards(): lower = jnp.linalg.cholesky(gram)]
    pallas_call x0 -> x2, Pallas kernels: none -> 113 us  [the longest x1 84.8 us: shards(): pl.pallas_call(functools.partial(exchange_kernel, G, C, S * A * R), out_s...]
    all_to_all x1 -> x0, blocking collectives: 53.4 us -> none  [shards(): fibres = lax.all_to_all(proj, 'ga', split_axis=0, concat_axis=3, tiled=True)]
    all_gather x1 -> x0, blocking collectives: 29.8 us -> none  [shards(): whole_factor = lax.all_gather(factor, 'sa', axis=0, tiled=True)]
    another operation x17 -> x0, local copies, waits for them, and re-layouts: 14.3 us -> none
    another operation x13 -> x0, matrix products: 13.1 us -> none  [the longest x7 7.6 us: shards(): solved = jax.scipy.linalg.solve_triangular(lower, columns.T, lower=True)]
    dot_general x2 -> x0, matrix products: 6.5 us -> none  [the longest x1 4.57 us: shards(): jnp.dot(columns.T, columns, precision=lax.Precision.HIGHEST, preferred_el...]
  transfers between devices with their start and end apart: 2 -> 0, of which waited for: 1 -> 0; matrix products, arithmetic and copies ran while one was open for 1% -> 0% of each run, Pallas kernels for 0% -> 0%
where the time goes in v1:
time: 116 us
  Pallas kernels  113 us (97%)
  local copies, waits for them, and re-layouts  2.27 us (2%)
    pallas_call x1, Pallas kernels, shards(): pl.pallas_call(functools.partial(exchange_kernel, G, C, S * A * R), out_s...  84.8 us
    pallas_call x1, Pallas kernels, shards(): pl.pallas_call(solve_kernel, out_shape=(jax.ShapeDtypeStruct((order // G,...  28.4 us

profile of v1, /device:TPU:0, one launch (start us, length us, event | category | flops | bytes accessed | tf_op | source)
XLA Modules:
  0.0 116.1 jit_solution(13715615949782625688)
XLA Ops:
  0.6 0.0 copy-start
  0.6 1.6 %copy-done = f32[8,64,8,128]{3,2,1,0:T(8,128)S(1)} copy-done((f32[8,64,8,128]{3,2,1,0:T(8,128)S(1)}, f32[8,64,8,128]{3,2,1,0:T(8,128)}, u32[]{:S(2)}) %copy-start) | copy-done | bytes 2097176
  2.2 0.0 copy-start.1
  2.2 0.7 copy-done.1
  2.9 84.8 %shard_map.41 = (f32[2,8,64,512]{3,2,1,0:T(8,128)S(1)}, f32[1280,128]{1,0:T(8,128)S(1)}) custom-call(f32[8,64,8,128]{3,2,1,0:T(8,128)S(1)} %copy-done, f32[8,64]{1,0:T(8,128)S(1)} %copy-done.1), custom_call_target="tpu_custom_call" | custom-call | tf_op jit(solution)/shard_map/pallas_call | solution.py:263
  87.7 28.4 %shard_map.42 = (f32[128,512]{1,0:T(8,128)}, f32[1024,512]{1,0:T(8,128)}) custom-call(f32[1024,512]{1,0:T(8,128)S(1)} %bitcast.2, f32[1280,128]{1,0:T(8,128)S(1)} %get-tuple-element.7.gram), custom_call_target="tpu_custom_call" | custom-call | tf_op jit(solution)/shard_map/pallas_call | solution.py:289
Async XLA Ops:
  0.6 1.6 %copy-start = (f32[8,64,8,128]{3,2,1,0:T(8,128)S(1)}, f32[8,64,8,128]{3,2,1,0:T(8,128)}, u32[]{:S(2)}) copy-start(f32[8,64,8,128]{3,2,1,0:T(8,128)} %slab.1) | copy-start | bytes 6291460
  2.2 0.7 copy-start.1

commit v2 on v1

--- a/solution.py
+++ b/solution.py
@@ -12,6 +12,7 @@
 LANES = 128
 HALF = 64
 STEP = 4
+STRIDE = 11
 
 
 def tn(a, b):
@@ -32,7 +33,7 @@
 
 
 def exchange_kernel(
-    G, C, count,
+    G, C, parts, count,
     slab, factor, unfold, gram,
     fibres, whole_factor, acc, r1, s1, r2, s2, r3,
     a2a_send, a2a_recv, f_send, f_recv, own_sem,
@@ -66,54 +67,65 @@
     def factor_copy(d):
         return remote(factor, whole_factor.at[j_rows, :], f_send.at[d], f_recv.at[d], (g, lax.rem(c + d, C)))
 
-    def chunk(to):
-        return slab.at[pl.ds((to // C) * s_here, s_here), pl.ds(lax.rem(to, C) * a_here, a_here)]
-
-    def slab_copy(d):
-        to = lax.rem(me + d, D)
+    a_group = a_here // parts
+
+    def chunk(s, a, to):
+        return slab.at[(to // C) * s_here + s, pl.ds(lax.rem(to, C) * a_here + a, a_group)]
+
+    def landing(s, a):
+        return fibres.at[s, a:a + a_group, j_rows, k_cols]
+
+    groups = [(s, a) for s in range(s_here) for a in range(0, a_here, a_group)]
+
+    def slab_copy(q, d):
+        to = lax.rem(me + lax.rem(d * STRIDE, D), D)
         return remote(
-            chunk(to), fibres.at[:, :, j_rows, k_cols], a2a_send.at[d], a2a_recv.at[d], (to // C, lax.rem(to, C))
+            chunk(*groups[q], to), landing(*groups[q]), a2a_send.at[q * D + d], a2a_recv.at[q * D + d],
+            (to // C, lax.rem(to, C)),
         )
 
     @pl.loop(1, C)
     def _(d):
         factor_copy(d).start()
 
-    @pl.loop(1, D)
-    def _(d):
-        slab_copy(d).start()
-
-    own = pltpu.make_async_copy(chunk(me), fibres.at[:, :, j_rows, k_cols], own_sem)
-    own.start()
+    for q in range(len(groups)):
+        @pl.loop(1, D)
+        def _(d):
+            slab_copy(q, d).start()
+
+    own = [pltpu.make_async_copy(chunk(*at, me), landing(*at), own_sem.at[q]) for q, at in enumerate(groups)]
+    for copy in own:
+        copy.start()
     whole_factor[j_rows, :] = factor[...]
-    own.wait()
 
     @pl.loop(1, C)
     def _(d):
         factor_copy(d).wait()
 
-    @pl.loop(1, D)
-    def _(d):
-        slab_copy(d).wait()
-
-    @pl.loop(0, s_here * a_here)
-    def _(i):
-        s, a = i // a_here, lax.rem(i, a_here)
-        unfold[s, a] = tn(whole_factor[...], fibres[s, a])
-
-    columns = unfold[...].reshape(s_here * a_here * unfold.shape[2], order)
-    hi, lo = split(columns)
-    at = 0
-    for left in range(0, order, LANES):
-        low_hi, low_lo = hi[:, left:], lo[:, left:]
-        this_hi, this_lo = hi[:, left:left + LANES], lo[:, left:left + LANES]
-        contract = ((0,), (0,))
-        part = mul16(low_hi, this_lo, contract) + mul16(low_lo, this_hi, contract)
-        part = part + mul16(low_hi, this_hi, contract)
-        acc[at:at + order - left, :] = part
-        at += order - left
-    if at < acc.shape[0]:
-        acc[at:, :] = jnp.zeros((acc.shape[0] - at, LANES), jnp.float32)
+    packed = order * (order + LANES) // (2 * LANES)
+    if packed < acc.shape[0]:
+        acc[packed:, :] = jnp.zeros((acc.shape[0] - packed, LANES), jnp.float32)
+    contract = ((0,), (0,))
+    for q, (s, a) in enumerate(groups):
+        own[q].wait()
+
+        @pl.loop(1, D)
+        def _(d):
+            slab_copy(q, d).wait()
+
+        pieces = [tn(whole_factor[...], fibres[s, a + i]) for i in range(a_group)]
+        for i in range(a_group):
+            unfold[s, a + i] = pieces[i]
+        hi, lo = split(jnp.concatenate(pieces, axis=0))
+        at = 0
+        for left in range(0, order, LANES):
+            this_hi, this_lo = hi[:, left:left + LANES], lo[:, left:left + LANES]
+            part = mul16(hi[:, left:], this_lo, contract) + mul16(lo[:, left:], this_hi, contract)
+            part = part + mul16(hi[:, left:], this_hi, contract)
+            if q:
+                part = part + acc[at:at + order - left, :]
+            acc[at:at + order - left, :] = part
+            at += order - left
 
     half, quarter = s1.shape[0], s2.shape[0]
     eighth = quarter // G
@@ -258,10 +270,12 @@
     cut = 8 * 2 * chips * G
     packed = -(-(blocks * (blocks + 1) // 2 * LANES) // cut) * cut
     half, quarter = packed // 2, packed // 2 // chips
+    parts = 2 if a_here % 2 == 0 else 1
+    sends = s_here * parts * G * C
     f32 = jnp.float32
     dma = pltpu.SemaphoreType.DMA
     unfold, gram = pl.pallas_call(
-        functools.partial(exchange_kernel, G, C, S * A * R),
+        functools.partial(exchange_kernel, G, C, parts, S * A * R),
         out_shape=(
             jax.ShapeDtypeStruct((s_here, a_here, R, order), f32),
             jax.ShapeDtypeStruct((packed, LANES), f32),
@@ -277,7 +291,7 @@
             pltpu.VMEM((chips, quarter, LANES), f32),
             pltpu.VMEM((quarter, LANES), f32),
             pltpu.VMEM((G, quarter // G, LANES), f32),
-            dma((G * C,)), dma((G * C,)), dma((C,)), dma((C,)), dma,
+            dma((sends,)), dma((sends,)), dma((C,)), dma((C,)), dma((s_here * parts,)),
             dma, dma, dma((chips,)), dma((chips,)), dma((G,)), dma((G,)),
             dma((G,)), dma((G,)), dma((chips,)), dma((chips,)), dma, dma,
         ],

time: 116 us -> 110 us (0.948)
  Pallas kernels: 113 us -> 107 us
    pallas_call x1, Pallas kernels: 84.8 us -> 78.7 us  [shards(): pl.pallas_call(functools.partial(exchange_kernel, G, C, parts, S * A * R)...]
where the time goes in v2:
time: 110 us
  Pallas kernels  107 us (97%)
  local copies, waits for them, and re-layouts  2.27 us (2%)
    pallas_call x1, Pallas kernels, shards(): pl.pallas_call(functools.partial(exchange_kernel, G, C, parts, S * A * R)...  78.7 us
    pallas_call x1, Pallas kernels, shards(): pl.pallas_call(solve_kernel, out_shape=(jax.ShapeDtypeStruct((order // G,...  28.4 us
    unnamed x4, local copies, waits for them, and re-layouts  2.27 us

profile of v2, /device:TPU:0, one launch (start us, length us, event | category | flops | bytes accessed | tf_op | source)
XLA Modules:
  0.0 110.0 jit_solution(11157920754702303396)
XLA Ops:
  0.6 0.0 copy-start
  0.6 1.6 %copy-done = f32[8,64,8,128]{3,2,1,0:T(8,128)S(1)} copy-done((f32[8,64,8,128]{3,2,1,0:T(8,128)S(1)}, f32[8,64,8,128]{3,2,1,0:T(8,128)}, u32[]{:S(2)}) %copy-start) | copy-done | bytes 2097176
  2.2 0.0 copy-start.1
  2.2 0.7 copy-done.1
  2.9 78.7 %shard_map.41 = (f32[2,8,64,512]{3,2,1,0:T(8,128)S(1)}, f32[1280,128]{1,0:T(8,128)S(1)}) custom-call(f32[8,64,8,128]{3,2,1,0:T(8,128)S(1)} %copy-done, f32[8,64]{1,0:T(8,128)S(1)} %copy-done.1), custom_call_target="tpu_custom_call" | custom-call | tf_op jit(solution)/shard_map/pallas_call | solution.py:277
  81.6 28.4 %shard_map.42 = (f32[128,512]{1,0:T(8,128)}, f32[1024,512]{1,0:T(8,128)}) custom-call(f32[1024,512]{1,0:T(8,128)S(1)} %bitcast.2, f32[1280,128]{1,0:T(8,128)S(1)} %get-tuple-element.7.gram), custom_call_target="tpu_custom_call" | custom-call | tf_op jit(solution)/shard_map/pallas_call | solution.py:303
Async XLA Ops:
  0.6 1.6 %copy-start = (f32[8,64,8,128]{3,2,1,0:T(8,128)S(1)}, f32[8,64,8,128]{3,2,1,0:T(8,128)}, u32[]{:S(2)}) copy-start(f32[8,64,8,128]{3,2,1,0:T(8,128)} %slab.1) | copy-start | bytes 6291460
  2.2 0.7 copy-start.1

commit v3 on v2

--- a/solution.py
+++ b/solution.py
@@ -11,7 +11,7 @@
 HIGHEST = lax.Precision.HIGHEST
 LANES = 128
 HALF = 64
-STEP = 4
+STEP = 8
 STRIDE = 11
 
 
@@ -224,8 +224,10 @@
     return u, w
 
 
-def solve_kernel(unfold, gram, lower, basis, upper, inverse):
+def solve_kernel(unfold, gram, lower, basis, upper, inverse, x_hi, x_lo, out, out_sem):
     order = upper.shape[0]
+    x_hi[...], x_lo[...] = split(unfold[...])
+    copies = []
     upper[...] = jnp.zeros_like(upper)
     inverse[...] = jnp.zeros_like(inverse)
     at = 0
@@ -240,6 +242,13 @@
         if i:
             inverse[i:n, :i] = nn(w, inverse[i:n, :i])
         inverse[i:n, i:n] = w
+        w_hi, w_lo = split(inverse[i:n, :n])
+        contract = ((1,), (1,))
+        part = mul16(x_hi[:, :n], w_lo, contract) + mul16(x_lo[:, :n], w_hi, contract)
+        b = i // LANES
+        out[b] = part + mul16(x_hi[:, :n], w_hi, contract)
+        copies.append(pltpu.make_async_copy(out.at[b], basis.at[:, i:n], out_sem.at[b]))
+        copies[-1].start()
         if n < order:
             right = nn(w, upper[i:n, n:])
             upper[i:n, n:] = right
@@ -250,15 +259,8 @@
     g = lax.axis_index("ga")
     mine = lower.shape[0]
     lower[...] = upper[:, pl.ds(pl.multiple_of(g * mine, mine), mine)].T
-    w_hi, w_lo = split(inverse[...])
-    contract = ((1,), (1,))
-
-    @pl.loop(0, basis.shape[0] // LANES)
-    def _(r):
-        here = pl.ds(pl.multiple_of(r * LANES, LANES), LANES)
-        hi, lo = split(unfold[here, :])
-        out = mul16(hi, w_lo, contract) + mul16(lo, w_hi, contract)
-        basis[here, :] = out + mul16(hi, w_hi, contract)
+    for copy in copies:
+        copy.wait()
 
 
 def shards(G, C, slab, factor):
@@ -307,8 +309,15 @@
             jax.ShapeDtypeStruct((rows, order), f32),
         ),
         in_specs=[pl.BlockSpec(memory_space=pltpu.VMEM)] * 2,
-        out_specs=(pl.BlockSpec(memory_space=pltpu.VMEM), pl.BlockSpec(memory_space=pltpu.VMEM)),
-        scratch_shapes=[pltpu.VMEM((order, order), f32), pltpu.VMEM((order, order), f32)],
+        out_specs=(pl.BlockSpec(memory_space=pltpu.VMEM), pl.BlockSpec(memory_space=pl.ANY)),
+        scratch_shapes=[
+            pltpu.VMEM((order, order), f32),
+            pltpu.VMEM((order, order), f32),
+            pltpu.VMEM((rows, order), jnp.bfloat16),
+            pltpu.VMEM((rows, order), jnp.bfloat16),
+            pltpu.VMEM((blocks, rows, LANES), f32),
+            dma((blocks,)),
+        ],
         compiler_params=pltpu.CompilerParams(vmem_limit_bytes=40 * 1024 * 1024),
     )(unfold.reshape(rows, order), gram)
     return lower, basis.reshape(s_here, a_here, R, order)

time: 110 us -> 105 us (0.955)
  Pallas kernels: 107 us -> 102 us
    pallas_call x1, Pallas kernels: 28.4 us -> 23.3 us  [shards(): pl.pallas_call(solve_kernel, out_shape=(jax.ShapeDtypeStruct((order // G,...]
where the time goes in v3:
time: 105 us
  Pallas kernels  102 us (97%)
  local copies, waits for them, and re-layouts  2.27 us (2%)
    pallas_call x1, Pallas kernels, shards(): pl.pallas_call(functools.partial(exchange_kernel, G, C, parts, S * A * R)...  78.7 us
    pallas_call x1, Pallas kernels, shards(): pl.pallas_call(solve_kernel, out_shape=(jax.ShapeDtypeStruct((order // G,...  23.3 us
    unnamed x4, local copies, waits for them, and re-layouts  2.27 us

profile of v3, /device:TPU:0, one launch (start us, length us, event | category | flops | bytes accessed | tf_op | source)
XLA Modules:
  0.0 105.1 jit_solution(12325149623797038497)
XLA Ops:
  0.6 0.0 copy-start
  0.6 1.6 %copy-done = f32[8,64,8,128]{3,2,1,0:T(8,128)S(1)} copy-done((f32[8,64,8,128]{3,2,1,0:T(8,128)S(1)}, f32[8,64,8,128]{3,2,1,0:T(8,128)}, u32[]{:S(2)}) %copy-start) | copy-done | bytes 2097176
  2.2 0.0 copy-start.1
  2.2 0.7 copy-done.1
  2.9 78.7 %shard_map.41 = (f32[2,8,64,512]{3,2,1,0:T(8,128)S(1)}, f32[1280,128]{1,0:T(8,128)S(1)}) custom-call(f32[8,64,8,128]{3,2,1,0:T(8,128)S(1)} %copy-done, f32[8,64]{1,0:T(8,128)S(1)} %copy-done.1), custom_call_target="tpu_custom_call" | custom-call | tf_op jit(solution)/shard_map/pallas_call | solution.py:279
  81.6 23.3 %shard_map.42 = (f32[128,512]{1,0:T(8,128)}, f32[1024,512]{1,0:T(8,128)}) custom-call(f32[1024,512]{1,0:T(8,128)S(1)} %bitcast.2, f32[1280,128]{1,0:T(8,128)S(1)} %get-tuple-element.7.gram), custom_call_target="tpu_custom_call" | custom-call | tf_op jit(solution)/shard_map/pallas_call | solution.py:305
Async XLA Ops:
  0.6 1.6 %copy-start = (f32[8,64,8,128]{3,2,1,0:T(8,128)S(1)}, f32[8,64,8,128]{3,2,1,0:T(8,128)}, u32[]{:S(2)}) copy-start(f32[8,64,8,128]{3,2,1,0:T(8,128)} %slab.1) | copy-start | bytes 6291460
  2.2 0.7 copy-start.1

commit v4 on v3

--- a/solution.py
+++ b/solution.py
@@ -134,17 +134,26 @@
         return pl.ds(pl.multiple_of(start, 8), size)
 
     partner = (g, c + 1 - 2 * core)
-    swap = remote(acc.at[rows((1 - core) * half, half)], r1, p1_send, p1_recv, partner)
-    swap.start()
-    swap.wait()
-    s1[...] = acc[rows(core * half, half), :] + r1[...]
+
+    def swap(d):
+        here = lax.rem(chip + d, chips) * quarter
+        return remote(
+            acc.at[rows((1 - core) * half + here, quarter)], r1.at[rows(here, quarter)],
+            p1_send.at[d], p1_recv.at[d], partner,
+        )
 
     def plane(d):
         to = lax.rem(chip + d, chips)
         return remote(s1.at[rows(to * quarter, quarter)], r2.at[d], p2_send.at[d], p2_recv.at[d], (g, to * 2 + core))
 
-    for d in range(1, chips):
-        plane(d).start()
+    for d in range(1, chips + 1):
+        swap(d % chips).start()
+    for d in range(1, chips + 1):
+        swap(d % chips).wait_recv()
+        here = lax.rem(chip + d, chips) * quarter
+        s1[rows(here, quarter), :] = acc[rows(core * half + here, quarter), :] + r1[rows(here, quarter), :]
+        if d < chips:
+            plane(d).start()
     for d in range(1, chips):
         plane(d).wait()
     total = s1[rows(chip * quarter, quarter), :]
@@ -169,24 +178,40 @@
     def line_back(d):
         return remote(gram.at[mine], gram.at[mine], g1_send.at[d], g1_recv.at[d], (lax.rem(g + d, G), c))
 
+    def piece(z, d):
+        owner = lax.rem(chip - d + chips, chips)
+        return rows(core * half + owner * quarter + lax.rem(g - z + G, G) * eighth, eighth)
+
+    def plane_back(z, d):
+        to = lax.rem(chip + d, chips)
+        sem = z * chips + d
+        return remote(gram.at[piece(z, 0)], gram.at[piece(z, 0)], g2_send.at[sem], g2_recv.at[sem], (g, to * 2 + core))
+
+    def swap_back(z, d):
+        sem = z * chips + d
+        return remote(gram.at[piece(z, d)], gram.at[piece(z, d)], g3_send.at[sem], g3_recv.at[sem], partner)
+
     for d in range(1, G):
         line_back(d).start()
-    for d in range(1, G):
-        line_back(d).wait()
-    mine2 = rows(core * half + chip * quarter, quarter)
-
-    def plane_back(d):
-        to = lax.rem(chip + d, chips)
-        return remote(gram.at[mine2], gram.at[mine2], g2_send.at[d], g2_recv.at[d], (g, to * 2 + core))
-
-    for d in range(1, chips):
-        plane_back(d).start()
-    for d in range(1, chips):
-        plane_back(d).wait()
-    mine3 = rows(core * half, half)
-    swap_back = remote(gram.at[mine3], gram.at[mine3], g3_send, g3_recv, partner)
-    swap_back.start()
-    swap_back.wait()
+    for z in range(G):
+        if z:
+            line_back(z).wait_recv()
+        for d in range(1, chips):
+            plane_back(z, d).start()
+        swap_back(z, 0).start()
+    for z in range(G):
+        for d in range(1, chips):
+            plane_back(z, d).wait_recv()
+            swap_back(z, d).start()
+    for d in range(1, G):
+        line_back(d).wait_send()
+    for d in range(chips):
+        swap(d).wait_send()
+    for z in range(G):
+        for d in range(chips):
+            if d:
+                plane_back(z, d).wait_send()
+            swap_back(z, d).wait()
 
 
 def eliminate(block):
@@ -294,8 +319,8 @@
             pltpu.VMEM((quarter, LANES), f32),
             pltpu.VMEM((G, quarter // G, LANES), f32),
             dma((sends,)), dma((sends,)), dma((C,)), dma((C,)), dma((s_here * parts,)),
-            dma, dma, dma((chips,)), dma((chips,)), dma((G,)), dma((G,)),
-            dma((G,)), dma((G,)), dma((chips,)), dma((chips,)), dma, dma,
+            dma((chips,)), dma((chips,)), dma((chips,)), dma((chips,)), dma((G,)), dma((G,)),
+            dma((G,)), dma((G,)), *(dma((G * chips,)) for _ in range(4)),
         ],
         compiler_params=pltpu.CompilerParams(
             collective_id=0, has_side_effects=True, vmem_limit_bytes=40 * 1024 * 1024

time: 105 us -> 105 us (level)
  no operation moved by 1% of the time
where the time goes in v4:
time: 105 us; the launch traced here: 104 us
  Pallas kernels  101 us (96%)
  local copies, waits for them, and re-layouts  2.27 us (2%)
    pallas_call x1, Pallas kernels, shards(): pl.pallas_call(functools.partial(exchange_kernel, G, C, parts, S * A * R)...  78 us
    pallas_call x1, Pallas kernels, shards(): pl.pallas_call(solve_kernel, out_shape=(jax.ShapeDtypeStruct((order // G,...  23.3 us
    unnamed x4, local copies, waits for them, and re-layouts  2.27 us

profile of v4, /device:TPU:0, one launch (start us, length us, event | category | flops | bytes accessed | tf_op | source)
XLA Modules:
  0.0 104.3 jit_solution(7444445113393595640)
XLA Ops:
  0.6 0.0 copy-start
  0.6 1.6 %copy-done = f32[8,64,8,128]{3,2,1,0:T(8,128)S(1)} copy-done((f32[8,64,8,128]{3,2,1,0:T(8,128)S(1)}, f32[8,64,8,128]{3,2,1,0:T(8,128)}, u32[]{:S(2)}) %copy-start) | copy-done | bytes 2097176
  2.2 0.0 copy-start.1
  2.2 0.7 copy-done.1
  2.9 78.0 %shard_map.41 = (f32[2,8,64,512]{3,2,1,0:T(8,128)S(1)}, f32[1280,128]{1,0:T(8,128)S(1)}) custom-call(f32[8,64,8,128]{3,2,1,0:T(8,128)S(1)} %copy-done, f32[8,64]{1,0:T(8,128)S(1)} %copy-done.1), custom_call_target="tpu_custom_call" | custom-call | tf_op jit(solution)/shard_map/pallas_call | solution.py:304
  80.9 23.3 %shard_map.42 = (f32[128,512]{1,0:T(8,128)}, f32[1024,512]{1,0:T(8,128)}) custom-call(f32[1024,512]{1,0:T(8,128)S(1)} %bitcast.2, f32[1280,128]{1,0:T(8,128)S(1)} %get-tuple-element.7.gram), custom_call_target="tpu_custom_call" | custom-call | tf_op jit(solution)/shard_map/pallas_call | solution.py:330
Async XLA Ops:
  0.6 1.6 %copy-start = (f32[8,64,8,128]{3,2,1,0:T(8,128)S(1)}, f32[8,64,8,128]{3,2,1,0:T(8,128)}, u32[]{:S(2)}) copy-start(f32[8,64,8,128]{3,2,1,0:T(8,128)} %slab.1) | copy-start | bytes 6291460
  2.2 0.7 copy-start.1
